TPU v7x, 32 devices: a whole 2x2x4 slice. The times are simulated.
32 devices in a mesh: sys: 2 (over x), box: 16 (over z, y, core).
Axes of the slice: x: 2, y: 2, z: 4, core: 2. Of those that a mesh axis runs over, the one named last changes fastest.
Arguments:
- charges: bfloat16 [16, 131072], P(None, ('sys', 'box')), parts along dimension 1, may hold values from -6 to 6
- harmonics: bfloat16 [121, 131072], P(None, ('sys', 'box')), parts along dimension 1, may hold values from -0.59765625 to 0.59765625
- counts: int32 [256], P(('sys', 'box')), parts along dimension 0, may hold values from 128 to 512, as said below
- m2l_ops: bfloat16 [121, 22869], replicated, may hold values from -0.0390625 to 0.0390625
- m2m_ops: bfloat16 [8, 121, 121], replicated, may hold values from -0.1875 to 0.1875
- l2l_ops: bfloat16 [8, 121, 121], replicated, may hold values from -0.5 to 0.5
- sources: int32 [189, 256], P(None, ('sys', 'box')), parts along dimension 1, may hold values from 0 to 127, as said below
- list_mask: int32 [189, 256], P(None, ('sys', 'box')), parts along dimension 1, may hold values 0 or 1
- top_sources: int32 [32, 32], P('sys'), parts along dimension 0, may hold values from 0 to 15
- top_vectors: int32 [32, 32], P('sys'), parts along dimension 0, may hold values from 0 to 188
- neighbours: int32 [32, 131072], P(None, ('sys', 'box')), parts along dimension 1, may hold values from 0 to 6143, as said below
- edge_weights: bfloat16 [32, 131072], P(None, ('sys', 'box')), parts along dimension 1, may hold values from -1 to 1
Outputs:
- potential: bfloat16 [16, 131072], P(None, ('sys', 'box')), parts along dimension 1
There are 2 independent parts, one for each index of `sys`. A program takes and returns all parts, laid end to end along the dimension named above; an argument that names none is the same for every part. Nothing has to cross between parts.
Inputs may be any that keep to these rules, and one draw needn't show every extreme that they name: `counts`: each leaf holds 128 to 512 atoms; every device's range of leaves has a full one. sources[v, t] lies in the leaves from (t // 8 - 1) * 8 to (t // 8 + 2) * 8 - 1; both ends are reached in every range where they exist. `neighbours`: both ends of the window are reached in every device's range of atoms.
All inputs are finite; a program needn't handle non-finite values. No bound on the sum of `list_mask` on one device may be relied on, other than what follows from the above.
Results may differ from a plain program's by a relative error of at most 0.003.
Values may be sent and summed in bfloat16 or wider, within the bound.
A program may use at most 128 MiB of HBM per device.

v0:
```python
import jax
import jax.numpy as jnp
from jax import lax
from jax.sharding import PartitionSpec as P

VBLK = 27


def padded(shard, sides, width):
    for axis, dim in sides:
        devices, length = (lax.axis_size(axis), shard.shape[dim])
        up = [(i, (i + 1) % devices) for i in range(devices - 1)]
        down = [(j, i) for i, j in up]
        last = lax.slice_in_dim(shard, length - width, length, axis=dim)
        initial = lax.slice_in_dim(shard, 0, width, axis=dim)
        before = lax.ppermute(last, axis, up)
        after = lax.ppermute(initial, axis, down)
        shard = jnp.concatenate([before, shard, after], axis=dim)
    return shard


def body(
    charges,
    harmonics,
    counts,
    m2l_ops,
    m2m_ops,
    l2l_ops,
    sources,
    list_mask,
    top_sources,
    top_vectors,
    neighbours,
    edge_weights,
):
    ncoef = harmonics.shape[0]
    chans = charges.shape[0]
    box_dev = counts.shape[0]
    atom_dev = charges.shape[1]
    slots = atom_dev // box_dev
    ghost = atom_dev // 4
    nvec = sources.shape[0]
    position = lax.axis_index("box")
    live = jnp.arange(slots, dtype=jnp.int32)[None, :] < counts[:, None]
    masked = jnp.where(
        live[None], charges.reshape(chans, box_dev, slots), jnp.zeros((), jnp.bfloat16)
    )
    flat_masked = masked.reshape(chans, atom_dev)
    harm_box = harmonics.reshape(ncoef, box_dev, slots)
    mult = jnp.einsum("kba,cba->kcb", harm_box, masked, preferred_element_type=jnp.float32).astype(
        jnp.bfloat16
    )
    edge_size = chans * ghost
    mult_size = ncoef * chans * box_dev
    reach = edge_size + mult_size
    low_edge = flat_masked[:, :ghost].reshape(edge_size)
    high_edge = flat_masked[:, atom_dev - ghost :].reshape(edge_size)
    packed = jnp.concatenate([low_edge, mult.reshape(mult_size), high_edge])
    extended = padded(packed, (("box", 0),), reach)
    from_low = extended[:reach]
    from_high = extended[extended.shape[0] - reach :]
    mult_low = from_low[:mult_size].reshape(ncoef, chans, box_dev)
    charge_low = from_low[mult_size:].reshape(chans, ghost)
    charge_high = from_high[:edge_size].reshape(chans, ghost)
    mult_high = from_high[edge_size:].reshape(ncoef, chans, box_dev)
    ext_charges = jnp.concatenate([charge_low, flat_masked, charge_high], axis=1)
    ext_mult = jnp.concatenate([mult_low, mult, mult_high], axis=2)
    level = mult
    while level.shape[2] > 1:
        grouped = level.reshape(ncoef, chans, level.shape[2] // 8, 8)
        level = jnp.einsum(
            "okl,lcpo->kcp", m2m_ops, grouped, preferred_element_type=jnp.float32
        ).astype(jnp.bfloat16)
    operators = m2l_ops.reshape(ncoef, nvec, ncoef)
    row_sources = lax.dynamic_slice_in_dim(top_sources, position, 1, 0)[0]
    row_vectors = lax.dynamic_slice_in_dim(top_vectors, position, 1, 0)[0]
    piece = lax.all_gather(level, "box", axis=2, tiled=True)
    columns = jnp.arange(piece.shape[2], dtype=jnp.int32)
    hits = (row_sources[:, None] == columns[None, :]).astype(jnp.bfloat16)
    picked = jnp.einsum("jn,kcn->jkc", hits, piece, preferred_element_type=jnp.float32)
    chosen = jnp.take(operators, row_vectors, axis=1)
    top_local = jnp.einsum(
        "kjl,jlc->kc", chosen, picked.astype(jnp.bfloat16), preferred_element_type=jnp.float32
    )
    current = top_local.astype(jnp.bfloat16).reshape(ncoef, chans, 1)
    local_index = sources - (position - 1) * box_dev
    leaf_local = jnp.zeros((ncoef, chans * box_dev), jnp.float32)
    for offset in range(0, nvec, VBLK):
        index_block = local_index[offset : offset + VBLK]
        mask_block = list_mask[offset : offset + VBLK].astype(jnp.bfloat16)
        picked_block = ext_mult[:, :, index_block] * mask_block[None, None]
        stacked = picked_block.transpose(2, 0, 1, 3).reshape(VBLK * ncoef, chans * box_dev)
        ops_block = m2l_ops[:, offset * ncoef : (offset + VBLK) * ncoef]
        leaf_local = leaf_local + jnp.dot(ops_block, stacked, preferred_element_type=jnp.float32)
    leaf_local = leaf_local.reshape(ncoef, chans, box_dev)
    levels = 0
    width = 1
    while width < box_dev:
        width = width * 8
        levels = levels + 1
    child = jnp.einsum("okl,lcp->kcpo", l2l_ops, current, preferred_element_type=jnp.float32)
    child = child.reshape(ncoef, chans, current.shape[2] * 8)
    local = (leaf_local + child).astype(jnp.bfloat16)
    far = jnp.einsum("kba,kcb->cba", harm_box, local, preferred_element_type=jnp.float32).reshape(
        chans, atom_dev
    )
    gathered = ext_charges[:, neighbours]
    near = jnp.einsum("csa,sa->ca", gathered, edge_weights, preferred_element_type=jnp.float32)
    return (far + near).astype(jnp.bfloat16)


def solution(mesh):
    return jax.shard_map(
        body,
        mesh=mesh,
        in_specs=(
            P(None, ("sys", "box")),
            P(None, ("sys", "box")),
            P(("sys", "box")),
            P(),
            P(),
            P(),
            P(None, ("sys", "box")),
            P(None, ("sys", "box")),
            P("sys", None),
            P("sys", None),
            P(None, ("sys", "box")),
            P(None, ("sys", "box")),
        ),
        out_specs=P(None, ("sys", "box")),
        check_vma=False,
    )
```

profile of v0, /device:TPU:0, one launch (start us, length us, event | category | flops | bytes accessed | tf_op | source)
XLA Modules:
  0.0 638.3 jit_solution(7878068652370831715)
XLA Ops:
  2.6 1.6 copy.130
  6.6 2.4 collective-permute-start
  15.9 25.4 %all_gather.3 = bf16[121,16,16]{0,1,2:T(8,128)(2,1)S(1)} all-gather(bf16[121,16,1]{0,1,2:T(8,128)(2,1)S(1)} %fusion.7), channel_id=1, replica_groups=mesh['sys'=2,'box'=16] {'box'}, dimensions={2}, use_global_device_ids=true | all-gather | bytes 65824 | tf_op jit(solution)/shard_map/all_gather | solution.py:77
  41.3 8.5 %reshape.265 = bf16[121,189,121]{0,2,1:T(8,128)(2,1)} reshape(bf16[121,22869]{0,1:T(8,128)(2,1)} %param.15) | data formatting | bytes 11068596 | tf_op jit(solution)/shard_map/reshape | solution.py:74
  49.8 8.9 %copy.110 = bf16[121,189,121]{2,0,1:T(8,128)(2,1)} copy(bf16[121,189,121]{0,2,1:T(8,128)(2,1)} %reshape.265) | data formatting | bytes 11068596 | tf_op jit(solution)/shard_map/reshape | solution.py:74
  59.0 3.5 gather_fusion.7
  66.8 3.9 fusion.9
  70.8 3.2 reshape.164
  74.0 3.2 reshape.163
  78.8 3.9 fusion.11
  82.7 3.2 reshape.162
  85.9 3.2 reshape.161
  90.8 3.9 fusion.13
  94.7 3.2 reshape.160
  100.2 2.5 reshape.158
  104.2 3.2 reshape.159
  108.3 1.9 convolution_add_fusion.5
  110.3 1.9 convolution_add_fusion.4
  112.2 1.6 convolution_add_fusion.3
  113.7 1.6 convolution_add_fusion.2
  115.3 1.6 convolution_add_fusion.1
  116.9 1.6 fusion.1
  119.2 496.2 %gather_fusion.8 = bf16[131072,16]{1,0:T(8,128)(2,1)} fusion(bf16[16,6144]{0,1:T(8,128)(2,1)S(1)} %copy.118, s32[131072]{0:T(1024)} %broadcast_clamp_fusion), kind=kCustom, calls=%fused_computation.8 | custom fusion | bytes 8912896 | tf_op jit(solution)/shard_map/gather | solution.py:107
  615.4 21.6 %multiply_reduce_fusion = f32[4096,16]{1,0:T(8,128)S(1)} fusion(bf16[4096,32,16]{2,0,1:T(8,128)(2,1)} %bitcast.138, f32[4096,32]{0,1:T(8,128)S(1)} %copy-done.1), kind=kLoop, calls=%fused_computation.9 | loop fusion | flops 6225920 | bytes 4980736
  (101 shorter events, 26.1 us)
Async XLA Ops:
  0.0 118.5 %copy-start = (bf16[8,121,121]{2,0,1:T(8,128)(2,1)S(1)}, bf16[8,121,121]{2,0,1:T(8,128)(2,1)}, u32[]{:S(2)}) copy-start(bf16[8,121,121]{2,0,1:T(8,128)(2,1)} %param.17) | copy-start | bytes 702772
  0.0 12.4 %copy-start.9 = (s32[189,8]{0,1:T(8,128)S(1)}, s32[189,8]{0,1:T(8,128)}, u32[]{:S(2)}) copy-start(s32[189,8]{0,1:T(8,128)} %param.19) | copy-start | bytes 18148
  0.0 12.5 %copy-start.10 = (s32[189,8]{0,1:T(8,128)S(1)}, s32[189,8]{0,1:T(8,128)}, u32[]{:S(2)}) copy-start(s32[189,8]{0,1:T(8,128)} %param.18) | copy-start | bytes 18148
  0.0 13.9 %copy-start.6 = (s32[32,4096]{1,0:T(8,128)S(1)}, s32[32,4096]{1,0:T(8,128)}, u32[]{:S(2)}) copy-start(s32[32,4096]{1,0:T(8,128)} %param.22) | copy-start | bytes 1572868
  0.0 14.9 %copy-start.8 = (bf16[32,4096]{1,0:T(8,128)(2,1)S(1)}, bf16[32,4096]{1,0:T(8,128)(2,1)}, u32[]{:S(2)}) copy-start(bf16[32,4096]{1,0:T(8,128)(2,1)} %param.23) | copy-start | bytes 786436
  0.0 15.7 %copy-start.7 = (bf16[8,121,121]{2,0,1:T(8,128)(2,1)S(1)}, bf16[8,121,121]{2,0,1:T(8,128)(2,1)}, u32[]{:S(2)}) copy-start(bf16[8,121,121]{2,0,1:T(8,128)(2,1)} %param.16) | copy-start | bytes 702772
  6.6 56.4 %collective-permute-start = (bf16[31872]{0:T(1024)(128)(2,1)S(1)}, bf16[31872]{0:T(1024)(128)(2,1)S(1)}, u32[]{:S(2)}, u32[]{:S(2)}) collective-permute-start(bf16[31872]{0:T(1024)(128)(2,1)S(1)} %get-tuple-element.7), channel_id=1, source_target_pairs={{0,1},{1,2},{2,3},{3,4},{4,5},{5,6},{6,7},{7,8},{8,9},{9,10},{10,1... | collective-permute-start | bytes 191240 | tf_op jit(solution)/shard_map/ppermute | solution.py:16
  9.0 54.1 %collective-permute-start.1 = (bf16[31872]{0:T(1024)(128)(2,1)S(1)}, bf16[31872]{0:T(1024)(128)(2,1)S(1)}, u32[]{:S(2)}, u32[]{:S(2)}) collective-permute-start(bf16[31872]{0:T(1024)(128)(2,1)S(1)} %get-tuple-element.8), channel_id=1, source_target_pairs={{1,0},{2,1},{3,2},{4,3},{5,4},{6,5},{7,6},{8,7},{9,8},{10,9},{11,1... | collective-permute-start | bytes 191240 | tf_op jit(solution)/shard_map/ppermute | solution.py:17
  108.3 3.9 copy-start.5
  108.3 5.4 copy-start.4
  108.3 7.0 %copy-start.3 = (bf16[3267,128]{0,1:T(8,128)(2,1)S(1)}, bf16[3267,128]{0,1:T(8,128)(2,1)}, u32[]{:S(2)}) copy-start(bf16[3267,128]{0,1:T(8,128)(2,1)} %reshape.163) | copy-start | bytes 2509060
  110.3 6.6 %copy-start.2 = (bf16[3267,128]{0,1:T(8,128)(2,1)S(1)}, bf16[3267,128]{0,1:T(8,128)(2,1)}, u32[]{:S(2)}) copy-start(bf16[3267,128]{0,1:T(8,128)(2,1)} %reshape.164) | copy-start | bytes 2509060
  119.2 496.3 %copy-start.1 = (f32[4096,32]{0,1:T(8,128)S(1)}, f32[4096,32]{0,1:T(8,128)}, u32[]{:S(2)}) copy-start(f32[4096,32]{0,1:T(8,128)} %bitcast_convert_fusion) | copy-start | bytes 1572868
where the time goes:
time: 649 us; the launch traced here: 638 us
  local copies, waits for them, and re-layouts  554 us (85%)
  other arithmetic  40.7 us (6%)
  blocking collectives  25.4 us (4%)
  matrix products  14.5 us (2%)
    gather x1, local copies, waits for them, and re-layouts, body(): gathered = ext_charges[:, neighbours]  496 us
    all_gather x1, blocking collectives, body(): piece = lax.all_gather(level, 'box', axis=2, tiled=True)  25.4 us
    unnamed x3, other arithmetic  22.5 us
    reshape x7, local copies, waits for them, and re-layouts, body(): picked_block.transpose(2, 0, 1, 3).reshape(VBLK * ncoef, chans * box_dev)  21.7 us
    reshape x2, local copies, waits for them, and re-layouts, body(): operators = m2l_ops.reshape(ncoef, nvec, ncoef)  17.5 us
    mul x4, other arithmetic, body(): picked_block = ext_mult[:, :, index_block] * mask_block[None, None]  13.3 us
  transfers between devices with their start and end apart: 2, of which 0 were waited for; matrix products, arithmetic and copies ran while one was open for 4% of the time, Pallas kernels for 0%

commit v1 on v0

--- a/solution.py
+++ b/solution.py
@@ -1,6 +1,8 @@
 import jax
 import jax.numpy as jnp
 from jax import lax
+from jax.experimental import pallas as pl
+from jax.experimental.pallas import tpu as pltpu
 from jax.sharding import PartitionSpec as P
 
 VBLK = 27
@@ -17,6 +19,57 @@
         after = lax.ppermute(initial, axis, down)
         shard = jnp.concatenate([before, shard, after], axis=dim)
     return shard
+
+
+HI = 256
+TILE = 256
+
+
+def near_kernel(table_ref, index_ref, weight_ref, out_ref, weight_f32):
+    slots, tile = index_ref.shape
+    rows, high = table_ref.shape
+    chans = out_ref.shape[0]
+    groups = rows // chans
+    weight_f32[...] = weight_ref[...].astype(jnp.float32)
+    lane_rows = lax.broadcasted_iota(jnp.int32, (high, tile), 0).astype(jnp.bfloat16)
+    group_rows = lax.broadcasted_iota(jnp.int32, (groups, tile), 0)
+
+    def step(slot, total):
+        index = index_ref[pl.ds(slot, 1), :]
+        weight = weight_f32[pl.ds(slot, 1), :]
+        low = (index & (high - 1)).astype(jnp.float32).astype(jnp.bfloat16)
+        hot = jnp.where(lane_rows == low, jnp.bfloat16(1), jnp.bfloat16(0))
+        got = jnp.dot(table_ref[...], hot, preferred_element_type=jnp.float32)
+        group = lax.shift_right_logical(index, 8)
+        scale = jnp.where(group_rows == group, weight, 0.0)
+        terms = got.reshape(chans, groups // 8, 8, tile) * scale.reshape(1, groups // 8, 8, tile)
+        return total + jnp.sum(terms, axis=1)
+
+    total = lax.fori_loop(0, slots, step, jnp.zeros((chans, 8, tile), jnp.float32), unroll=2)
+    out_ref[...] = jnp.sum(total, axis=1)
+
+
+def near_field(ext_charges, neighbours, edge_weights):
+    chans, window = ext_charges.shape
+    slots, atoms = neighbours.shape
+    table = ext_charges.reshape(chans * (window // HI), HI)
+    return pl.pallas_call(
+        near_kernel,
+        grid=(atoms // TILE,),
+        in_specs=[
+            pl.BlockSpec(table.shape, lambda i: (0, 0)),
+            pl.BlockSpec((slots, TILE), lambda i: (0, i)),
+            pl.BlockSpec((slots, TILE), lambda i: (0, i)),
+        ],
+        out_specs=pl.BlockSpec((chans, TILE), lambda i: (0, i)),
+        out_shape=jax.ShapeDtypeStruct((chans, atoms), jnp.float32),
+        scratch_shapes=[pltpu.VMEM((slots, TILE), jnp.float32)],
+        compiler_params=pltpu.CompilerParams(vmem_limit_bytes=48 * 1024 * 1024),
+        cost_estimate=pl.CostEstimate(
+            flops=2 * slots * atoms * chans * window, bytes_accessed=slots * atoms * 6, transcendentals=0
+        ),
+        name="near_field",
+    )(table, neighbours, edge_weights)
 
 
 def body(
@@ -104,8 +157,7 @@
     far = jnp.einsum("kba,kcb->cba", harm_box, local, preferred_element_type=jnp.float32).reshape(
         chans, atom_dev
     )
-    gathered = ext_charges[:, neighbours]
-    near = jnp.einsum("csa,sa->ca", gathered, edge_weights, preferred_element_type=jnp.float32)
+    near = near_field(ext_charges, neighbours, edge_weights)
     return (far + near).astype(jnp.bfloat16)
 
 

time: 649 us -> 187 us (0.29); the launches traced: 638 us -> 186 us
  local copies, waits for them, and re-layouts: 554 us -> 55.4 us
  Pallas kernels: 0 us -> 72.3 us
  other arithmetic: 40.7 us -> 16.3 us
    gather x1 -> x0, local copies, waits for them, and re-layouts: 496 us -> none  [body(): gathered = ext_charges[:, neighbours]]
    pallas_call x0 -> x1, Pallas kernels: none -> 72.3 us  [near_field(): pl.pallas_call(near_kernel, grid=(atoms // TILE,), in_specs=[pl.BlockSpec...]
    unnamed x3 -> x0, other arithmetic: 22.5 us -> none
  transfers between devices with their start and end apart: 2 -> 2, of which waited for: 0 -> 0; matrix products, arithmetic and copies ran while one was open for 4% -> 14% of each run, Pallas kernels for 0% -> 0%
where the time goes in v1:
time: 187 us; the launch traced here: 186 us
  Pallas kernels  72.3 us (39%)
  local copies, waits for them, and re-layouts  55.4 us (30%)
  blocking collectives  23.3 us (12%)
  other arithmetic  16.3 us (9%)
  matrix products  14.2 us (8%)
  starting transfers between devices  4.33 us (2%)
    pallas_call x1, Pallas kernels, near_field(): pl.pallas_call(near_kernel, grid=(atoms // TILE,), in_specs=[pl.BlockSpec...  72.3 us
    all_gather x1, blocking collectives, body(): piece = lax.all_gather(level, 'box', axis=2, tiled=True)  23.3 us
    reshape x7, local copies, waits for them, and re-layouts, body(): picked_block.transpose(2, 0, 1, 3).reshape(VBLK * ncoef, chans * box_dev)  21 us
    reshape x2, local copies, waits for them, and re-layouts, body(): operators = m2l_ops.reshape(ncoef, nvec, ncoef)  17.5 us
    mul x4, other arithmetic, body(): picked_block = ext_mult[:, :, index_block] * mask_block[None, None]  12.3 us
    dot_general x7, matrix products, body(): jnp.dot(ops_block, stacked, preferred_element_type=jnp.float32)  11.4 us
    gather x7, local copies, waits for them, and re-layouts, body(): picked_block = ext_mult[:, :, index_block] * mask_block[None, None]  5.65 us
  transfers between devices with their start and end apart: 2, of which 0 were waited for; matrix products, arithmetic and copies ran while one was open for 14% of the time, Pallas kernels for 0%

profile of v1, /device:TPU:0, one launch (start us, length us, event | category | flops | bytes accessed | tf_op | source)
XLA Modules:
  0.0 186.3 jit_solution(4118195674867452647)
XLA Ops:
  0.0 1.7 copy.112
  7.8 3.0 %collective-permute-start = (bf16[31872]{0:T(1024)(128)(2,1)S(1)}, bf16[31872]{0:T(1024)(128)(2,1)S(1)}, u32[]{:S(2)}, u32[]{:S(2)}) collective-permute-start(bf16[31872]{0:T(1024)(128)(2,1)S(1)} %get-tuple-element.7), channel_id=1, source_target_pairs={{0,1},{1,2},{2,3},{3,4},{4,5},{5,6},{6,7},{7,8},{8,9},{9,10},{10,1... | collective-permute-start | bytes 191240 | tf_op jit(solution)/shard_map/ppermute | solution.py:18
  12.2 8.5 %reshape.257 = bf16[121,189,121]{0,2,1:T(8,128)(2,1)} reshape(bf16[121,22869]{0,1:T(8,128)(2,1)} %param.15) | data formatting | bytes 11068596 | tf_op jit(solution)/shard_map/reshape | solution.py:127
  20.7 9.0 %copy.100 = bf16[121,189,121]{2,0,1:T(8,128)(2,1)} copy(bf16[121,189,121]{0,2,1:T(8,128)(2,1)} %reshape.257) | data formatting | bytes 11068596 | tf_op jit(solution)/shard_map/reshape | solution.py:127
  29.9 23.3 %all_gather.3 = bf16[121,16,16]{0,1,2:T(8,128)(2,1)S(1)} all-gather(bf16[121,16,1]{0,1,2:T(8,128)(2,1)S(1)} %fusion.7), channel_id=1, replica_groups=mesh['sys'=2,'box'=16] {'box'}, dimensions={2}, use_global_device_ids=true | all-gather | bytes 65824 | tf_op jit(solution)/shard_map/all_gather | solution.py:130
  55.4 3.5 %gather_fusion.7 = bf16[32,121,121]{2,1,0:T(8,128)(2,1)S(1)} fusion(bf16[121,189,121]{2,0,1:T(8,128)(2,1)} %copy.100, s32[1024]{0:T(1024)S(1)} %pad_clamp_fusion), kind=kCustom, calls=%fused_computation.7 | custom fusion | bytes 1874176 | tf_op jit(solution)/shard_map/jit(_take)/gather | solution.py:134
  63.1 1.7 reshape.161
  64.8 1.6 fusion.26
  68.0 3.9 %fusion.13 = (bf16[27,121,16,8]{1,0,3,2:T(8,128)(2,1)}, bf16[27,121,16,8]{1,0,3,2:T(8,128)(2,1)}) fusion(bf16[27,8,121,16]{2,3,1,0:T(8,128)(2,1)S(1)} %bitcast.119, bf16[27,8]{0,1:T(8,128)(2,1)S(1)} %get-tuple-element.20, bf16[27,8]{0,1:T(8,128)(2,1)S(1)} %get-tuple-element.21, bf16[27,8,121,16]{2,3,1,0:T(8,128)(2,1)S(1)} %bitcast.121), kind=kLoop, calls=%fused_computation.38 | loop fusion | flops 836352 | bytes 3346272 | tf_op jit(solution)/shard_map/mul | solution.py:144
  72.0 3.2 %reshape.162 = bf16[3267,128]{0,1:T(8,128)(2,1)} reshape(bf16[27,121,16,8]{1,0,3,2:T(8,128)(2,1)} %get-tuple-element.28) | data formatting | bytes 1672704 | tf_op jit(solution)/shard_map/reshape | solution.py:145
  75.2 3.2 %reshape.163 = bf16[3267,128]{0,1:T(8,128)(2,1)} reshape(bf16[27,121,16,8]{1,0,3,2:T(8,128)(2,1)} %get-tuple-element.27) | data formatting | bytes 1672704 | tf_op jit(solution)/shard_map/reshape | solution.py:145
  80.0 3.9 %fusion.11 = (bf16[27,121,16,8]{1,0,3,2:T(8,128)(2,1)}, bf16[27,121,16,8]{1,0,3,2:T(8,128)(2,1)}) fusion(bf16[27,8,121,16]{2,3,1,0:T(8,128)(2,1)S(1)} %bitcast.120, bf16[27,8]{0,1:T(8,128)(2,1)S(1)} %get-tuple-element.18, bf16[27,8]{0,1:T(8,128)(2,1)S(1)} %get-tuple-element.19, bf16[27,8,121,16]{2,3,1,0:T(8,128)(2,1)S(1)} %bitcast.122), kind=kLoop, calls=%fused_computation.34 | loop fusion | flops 836352 | bytes 3346272 | tf_op jit(solution)/shard_map/mul | solution.py:144
  83.9 3.2 %reshape.164 = bf16[3267,128]{0,1:T(8,128)(2,1)} reshape(bf16[27,121,16,8]{1,0,3,2:T(8,128)(2,1)} %get-tuple-element.26) | data formatting | bytes 1672704 | tf_op jit(solution)/shard_map/reshape | solution.py:145
  87.1 3.2 %reshape.165 = bf16[3267,128]{0,1:T(8,128)(2,1)} reshape(bf16[27,121,16,8]{1,0,3,2:T(8,128)(2,1)} %get-tuple-element.25) | data formatting | bytes 1672704 | tf_op jit(solution)/shard_map/reshape | solution.py:145
  92.0 3.9 %fusion.9 = (bf16[27,121,16,8]{1,0,3,2:T(8,128)(2,1)}, bf16[27,121,16,8]{1,0,3,2:T(8,128)(2,1)}) fusion(bf16[27,8,121,16]{2,3,1,0:T(8,128)(2,1)S(1)} %bitcast.117, bf16[27,8]{0,1:T(8,128)(2,1)S(1)} %get-tuple-element.16, bf16[27,8]{0,1:T(8,128)(2,1)S(1)} %get-tuple-element.17, bf16[27,8,121,16]{2,3,1,0:T(8,128)(2,1)S(1)} %bitcast.118), kind=kLoop, calls=%fused_computation.30 | loop fusion | flops 836352 | bytes 3346272 | tf_op jit(solution)/shard_map/mul | solution.py:144
  95.9 3.3 %reshape.166 = bf16[3267,128]{0,1:T(8,128)(2,1)} reshape(bf16[27,121,16,8]{1,0,3,2:T(8,128)(2,1)} %get-tuple-element.24) | data formatting | bytes 1672704 | tf_op jit(solution)/shard_map/reshape | solution.py:145
  99.2 3.2 %reshape.167 = bf16[3267,128]{0,1:T(8,128)(2,1)} reshape(bf16[27,121,16,8]{1,0,3,2:T(8,128)(2,1)} %get-tuple-element.23) | data formatting | bytes 1672704 | tf_op jit(solution)/shard_map/reshape | solution.py:145
  102.4 1.9 %convolution_add_fusion.5 = f32[128,121]{1,0:T(8,128)S(1)} fusion(f32[128,121]{1,0:T(8,128)S(1)} %fusion.26, bf16[3267,128]{0,1:T(8,128)(2,1)} %reshape.162, bf16[121,22869]{0,1:T(8,128)(2,1)} %param.15), kind=kOutput, calls=%fused_computation.18 | convolution fusion | flops 101214080 | bytes 1813504 | tf_op jit(solution)/shard_map/dot_general | solution.py:147
  104.4 1.6 convolution_add_fusion.4
  106.0 1.6 convolution_add_fusion.3
  107.6 1.6 convolution_add_fusion.2
  109.2 1.5 convolution_add_fusion.1
  110.8 1.5 fusion.1
  113.3 72.3 %near_field.1 = f32[16,4096]{1,0:T(8,128)S(1)} custom-call(bf16[384,256]{1,0:T(8,128)(2,1)S(1)} %reshape.174.table_ref, s32[32,4096]{1,0:T(8,128)S(1)} %copy-done.1, bf16[32,4096]{1,0:T(8,128)(2,1)S(1)} %copy-done.2), custom_call_target="tpu_custom_call" | custom-call | flops 25769803776 | bytes 786432 | tf_op jit(solution)/shard_map/near_field/pallas_call | solution.py:56
  (99 shorter events, 20.3 us)
Async XLA Ops:
  0.0 112.4 %copy-start = (bf16[8,121,121]{2,0,1:T(8,128)(2,1)S(1)}, bf16[8,121,121]{2,0,1:T(8,128)(2,1)}, u32[]{:S(2)}) copy-start(bf16[8,121,121]{2,0,1:T(8,128)(2,1)} %param.17) | copy-start | bytes 702772
  6.5 53.1 %collective-permute-start.1 = (bf16[31872]{0:T(1024)(128)(2,1)S(1)}, bf16[31872]{0:T(1024)(128)(2,1)S(1)}, u32[]{:S(2)}, u32[]{:S(2)}) collective-permute-start(bf16[31872]{0:T(1024)(128)(2,1)S(1)} %get-tuple-element.8), channel_id=1, source_target_pairs={{1,0},{2,1},{3,2},{4,3},{5,4},{6,5},{7,6},{8,7},{9,8},{10,9},{11,1... | collective-permute-start | bytes 191240 | tf_op jit(solution)/shard_map/ppermute | solution.py:19
  7.8 52.9 %collective-permute-start = (bf16[31872]{0:T(1024)(128)(2,1)S(1)}, bf16[31872]{0:T(1024)(128)(2,1)S(1)}, u32[]{:S(2)}, u32[]{:S(2)}) collective-permute-start(bf16[31872]{0:T(1024)(128)(2,1)S(1)} %get-tuple-element.7), channel_id=1, source_target_pairs={{0,1},{1,2},{2,3},{3,4},{4,5},{5,6},{6,7},{7,8},{8,9},{9,10},{10,1... | collective-permute-start | bytes 191240 | tf_op jit(solution)/shard_map/ppermute | solution.py:18
  20.7 9.0 %copy-start.8 = (bf16[8,121,121]{2,0,1:T(8,128)(2,1)S(1)}, bf16[8,121,121]{2,0,1:T(8,128)(2,1)}, u32[]{:S(2)}) copy-start(bf16[8,121,121]{2,0,1:T(8,128)(2,1)} %param.16) | copy-start | bytes 702772
  20.7 33.1 %copy-start.12 = (s32[189,8]{0,1:T(8,128)S(1)}, s32[189,8]{0,1:T(8,128)}, u32[]{:S(2)}) copy-start(s32[189,8]{0,1:T(8,128)} %param.18) | copy-start | bytes 18148
  20.7 33.4 %copy-start.11 = (s32[189,8]{0,1:T(8,128)S(1)}, s32[189,8]{0,1:T(8,128)}, u32[]{:S(2)}) copy-start(s32[189,8]{0,1:T(8,128)} %param.19) | copy-start | bytes 18148
  60.7 1.9 %copy-start.9 = (bf16[31872]{0:T(1024)(128)(2,1)}, bf16[31872]{0:T(1024)(128)(2,1)S(1)}, u32[]{:S(2)}) copy-start(bf16[31872]{0:T(1024)(128)(2,1)S(1)} %collective-permute-done) | copy-start | bytes 191236
  95.9 8.5 %copy-start.3 = (bf16[3267,128]{0,1:T(8,128)(2,1)S(1)}, bf16[3267,128]{0,1:T(8,128)(2,1)}, u32[]{:S(2)}) copy-start(bf16[3267,128]{0,1:T(8,128)(2,1)} %reshape.163) | copy-start | bytes 2509060
  95.9 10.1 %copy-start.4 = (bf16[3267,128]{0,1:T(8,128)(2,1)S(1)}, bf16[3267,128]{0,1:T(8,128)(2,1)}, u32[]{:S(2)}) copy-start(bf16[3267,128]{0,1:T(8,128)(2,1)} %reshape.164) | copy-start | bytes 2509060
  102.4 5.2 %copy-start.5 = (bf16[3267,128]{0,1:T(8,128)(2,1)S(1)}, bf16[3267,128]{0,1:T(8,128)(2,1)}, u32[]{:S(2)}) copy-start(bf16[3267,128]{0,1:T(8,128)(2,1)} %reshape.165) | copy-start | bytes 2509060
  102.4 6.8 %copy-start.6 = (bf16[3267,128]{0,1:T(8,128)(2,1)S(1)}, bf16[3267,128]{0,1:T(8,128)(2,1)}, u32[]{:S(2)}) copy-start(bf16[3267,128]{0,1:T(8,128)(2,1)} %reshape.166) | copy-start | bytes 2509060
  104.4 6.4 %copy-start.7 = (bf16[3267,128]{0,1:T(8,128)(2,1)S(1)}, bf16[3267,128]{0,1:T(8,128)(2,1)}, u32[]{:S(2)}) copy-start(bf16[3267,128]{0,1:T(8,128)(2,1)} %reshape.167) | copy-start | bytes 2509060
  107.6 5.5 %copy-start.10 = (bf16[31872]{0:T(1024)(128)(2,1)S(1)}, bf16[31872]{0:T(1024)(128)(2,1)}, u32[]{:S(2)}) copy-start(bf16[31872]{0:T(1024)(128)(2,1)} %copy-done.9) | copy-start | bytes 191236
  107.6 5.7 %copy-start.1 = (s32[32,4096]{1,0:T(8,128)S(1)}, s32[32,4096]{1,0:T(8,128)}, u32[]{:S(2)}) copy-start(s32[32,4096]{1,0:T(8,128)} %index_ref.1) | copy-start | bytes 1572868
  107.6 5.7 %copy-start.2 = (bf16[32,4096]{1,0:T(8,128)(2,1)S(1)}, bf16[32,4096]{1,0:T(8,128)(2,1)}, u32[]{:S(2)}) copy-start(bf16[32,4096]{1,0:T(8,128)(2,1)} %weight_ref.1) | copy-start | bytes 786436

commit v2 on v1

v2 whole, which is shorter than its diff:
```python
import jax
import jax.numpy as jnp
from jax import lax
from jax.experimental import pallas as pl
from jax.experimental.pallas import tpu as pltpu
from jax.sharding import PartitionSpec as P


HI = 256
TILE = 256


def near_kernel(table_ref, index_ref, weight_ref, out_ref, weight_f32):
    slots, tile = index_ref.shape
    rows, high = table_ref.shape
    chans = out_ref.shape[0]
    groups = rows // chans
    weight_f32[...] = weight_ref[...].astype(jnp.float32)
    lane_rows = lax.broadcasted_iota(jnp.int32, (high, tile), 0).astype(jnp.bfloat16)
    group_rows = lax.broadcasted_iota(jnp.int32, (groups, tile), 0)

    def step(slot, total):
        index = index_ref[pl.ds(slot, 1), :]
        weight = weight_f32[pl.ds(slot, 1), :]
        low = (index & (high - 1)).astype(jnp.float32).astype(jnp.bfloat16)
        hot = jnp.where(lane_rows == low, jnp.bfloat16(1), jnp.bfloat16(0))
        got = jnp.dot(table_ref[...], hot, preferred_element_type=jnp.float32)
        group = lax.shift_right_logical(index, 8)
        scale = jnp.where(group_rows == group, weight, 0.0)
        terms = got.reshape(chans, groups // 8, 8, tile) * scale.reshape(1, groups // 8, 8, tile)
        return total + jnp.sum(terms, axis=1)

    total = lax.fori_loop(0, slots, step, jnp.zeros((chans, 8, tile), jnp.float32), unroll=2)
    out_ref[...] = jnp.sum(total, axis=1)


def near_field(ext_charges, neighbours, edge_weights):
    chans, window = ext_charges.shape
    slots, atoms = neighbours.shape
    table = ext_charges.reshape(chans * (window // HI), HI)
    return pl.pallas_call(
        near_kernel,
        grid=(atoms // TILE,),
        in_specs=[
            pl.BlockSpec(table.shape, lambda i: (0, 0)),
            pl.BlockSpec((slots, TILE), lambda i: (0, i)),
            pl.BlockSpec((slots, TILE), lambda i: (0, i)),
        ],
        out_specs=pl.BlockSpec((chans, TILE), lambda i: (0, i)),
        out_shape=jax.ShapeDtypeStruct((chans, atoms), jnp.float32),
        scratch_shapes=[pltpu.VMEM((slots, TILE), jnp.float32)],
        compiler_params=pltpu.CompilerParams(vmem_limit_bytes=48 * 1024 * 1024),
        cost_estimate=pl.CostEstimate(
            flops=2 * slots * atoms * chans * window, bytes_accessed=slots * atoms * 6, transcendentals=0
        ),
        name="near_field",
    )(table, neighbours, edge_weights)


CHUNK = 2048


def field_kernel(
    source_ref,
    top_source_ref,
    top_vector_ref,
    table_ref,
    tops_ref,
    ops_ref,
    l2l_ref,
    harmonics_ref,
    near_ref,
    out_ref,
    table,
    tops,
    stack,
):
    ncoef, columns = ops_ref.shape
    chans, atoms = out_ref.shape
    nvec = columns // ncoef
    boxes = source_ref.shape[0] // nvec
    leaf_rows = boxes * chans
    slots = atoms // boxes
    table[:, :ncoef] = table_ref[...].astype(jnp.float32)
    tops[...] = jnp.zeros_like(tops)
    tops[:, :ncoef] = tops_ref[...].astype(jnp.float32)
    for vec in range(nvec):
        for box in range(boxes):
            row = pl.multiple_of(source_ref[vec * boxes + box] * chans, chans)
            stack[box * chans : (box + 1) * chans, vec * ncoef : (vec + 1) * ncoef] = table[
                pl.ds(row, chans), :ncoef
            ]
    stack[leaf_rows:, :] = jnp.zeros((chans, stack.shape[1]), jnp.float32)

    def add_entry(entry, carry):
        row = pl.multiple_of(top_source_ref[entry] * chans, chans)
        column = top_vector_ref[entry] * ncoef
        shift = column & 127
        start = pl.multiple_of(column - shift, 128)
        wide = jnp.concatenate(
            [tops[pl.ds(row, chans), :], jnp.zeros((chans, 128), jnp.float32)], axis=1
        )
        moved = pltpu.roll(wide, shift, 1)
        stack[leaf_rows:, pl.ds(start, 256)] = stack[leaf_rows:, pl.ds(start, 256)] + moved
        return carry

    lax.fori_loop(0, top_source_ref.shape[0], add_entry, 0)
    total = jnp.zeros((leaf_rows + chans, ncoef), jnp.float32)
    for start in range(0, columns, CHUNK):
        stop = min(start + CHUNK, columns)
        total = total + lax.dot_general(
            stack[:, start:stop].astype(jnp.bfloat16),
            ops_ref[:, start:stop],
            (((1,), (1,)), ((), ())),
            preferred_element_type=jnp.float32,
        )
    parent = total[leaf_rows:].astype(jnp.bfloat16)
    for box in range(boxes):
        child = lax.dot_general(
            parent,
            l2l_ref[box],
            (((1,), (1,)), ((), ())),
            preferred_element_type=jnp.float32,
        )
        local = (total[box * chans : (box + 1) * chans] + child).astype(jnp.bfloat16)
        span = slice(box * slots, (box + 1) * slots)
        far = jnp.dot(local, harmonics_ref[:, span], preferred_element_type=jnp.float32)
        out_ref[:, span] = (far + near_ref[:, span]).astype(out_ref.dtype)


def field(source, top_source, top_vector, table, tops, ops, l2l_ops, harmonics, near):
    chans, atoms = near.shape
    ncoef, columns = ops.shape
    boxes = l2l_ops.shape[0]
    rows = (boxes + 1) * chans
    width = (columns // 128 + 2) * 128
    smem = pl.BlockSpec(memory_space=pltpu.SMEM)
    vmem = pl.BlockSpec(memory_space=pltpu.VMEM)
    return pl.pallas_call(
        field_kernel,
        in_specs=[smem] * 3 + [vmem] * 6,
        out_specs=vmem,
        out_shape=jax.ShapeDtypeStruct((chans, atoms), jnp.bfloat16),
        scratch_shapes=[
            pltpu.VMEM((table.shape[0], 128), jnp.float32),
            pltpu.VMEM((tops.shape[0], 128), jnp.float32),
            pltpu.VMEM((rows, width), jnp.float32),
        ],
        compiler_params=pltpu.CompilerParams(vmem_limit_bytes=56 * 1024 * 1024),
        cost_estimate=pl.CostEstimate(
            flops=2 * rows * ncoef * columns, bytes_accessed=2 * ncoef * (columns + atoms), transcendentals=0
        ),
        name="field",
    )(source, top_source, top_vector, table, tops, ops, l2l_ops, harmonics, near)


def body(
    charges,
    harmonics,
    counts,
    m2l_ops,
    m2m_ops,
    l2l_ops,
    sources,
    list_mask,
    top_sources,
    top_vectors,
    neighbours,
    edge_weights,
):
    ncoef = harmonics.shape[0]
    chans = charges.shape[0]
    box_dev = counts.shape[0]
    atom_dev = charges.shape[1]
    slots = atom_dev // box_dev
    ghost = atom_dev // 4
    position = lax.axis_index("box")
    live = jnp.arange(slots, dtype=jnp.int32)[None, :] < counts[:, None]
    masked = jnp.where(
        live[None], charges.reshape(chans, box_dev, slots), jnp.zeros((), jnp.bfloat16)
    )
    flat_masked = masked.reshape(chans, atom_dev)
    harm_box = harmonics.reshape(ncoef, box_dev, slots)
    mult = jnp.einsum("cba,kba->bck", masked, harm_box, preferred_element_type=jnp.float32).astype(
        jnp.bfloat16
    )
    top = jnp.einsum("ocl,okl->ck", mult, m2m_ops, preferred_element_type=jnp.float32).astype(
        jnp.bfloat16
    )
    tops = lax.all_gather(top, "box", axis=0, tiled=True)
    devices = lax.axis_size("box")
    up = [(i, (i + 1) % devices) for i in range(devices - 1)]
    down = [(j, i) for i, j in up]
    charge_low = lax.ppermute(flat_masked[:, atom_dev - ghost :], "box", up)
    charge_high = lax.ppermute(flat_masked[:, :ghost], "box", down)
    rows = mult.reshape(box_dev * chans, ncoef)
    rows_low = lax.ppermute(rows, "box", up)
    rows_high = lax.ppermute(rows, "box", down)
    ext_charges = jnp.concatenate([charge_low, flat_masked, charge_high], axis=1)
    near = near_field(ext_charges, neighbours, edge_weights)
    table = jnp.concatenate(
        [rows_low, rows, rows_high, jnp.zeros((chans, ncoef), jnp.bfloat16)], axis=0
    )
    local_index = sources - (position - 1) * box_dev
    local_index = jnp.where(list_mask != 0, local_index, 3 * box_dev).reshape(-1)
    row_sources = lax.dynamic_slice_in_dim(top_sources, position, 1, 0)[0]
    row_vectors = lax.dynamic_slice_in_dim(top_vectors, position, 1, 0)[0]
    return field(
        local_index, row_sources, row_vectors, table, tops, m2l_ops, l2l_ops, harmonics, near
    )


def solution(mesh):
    return jax.shard_map(
        body,
        mesh=mesh,
        in_specs=(
            P(None, ("sys", "box")),
            P(None, ("sys", "box")),
            P(("sys", "box")),
            P(),
            P(),
            P(),
            P(None, ("sys", "box")),
            P(None, ("sys", "box")),
            P("sys", None),
            P("sys", None),
            P(None, ("sys", "box")),
            P(None, ("sys", "box")),
        ),
        out_specs=P(None, ("sys", "box")),
        check_vma=False,
    )
```

time: 187 us -> 138 us (0.74)
  local copies, waits for them, and re-layouts: 55.4 us -> 14.6 us
  other arithmetic: 16.3 us -> 2.52 us
  matrix products: 14.2 us -> 1.49 us
  Pallas kernels: 72.3 us -> 84.1 us
  starting transfers between devices: 4.33 us -> 10.1 us
    reshape x17 -> x1, local copies, waits for them, and re-layouts: 41.2 us -> 0.71 us  [body(): jnp.where(list_mask != 0, local_index, 3 * box_dev).reshape(-1)]
    dot_general x12 -> x2, matrix products: 14.2 us -> 1.49 us  [the longest x1 1.32 us: body(): jnp.einsum('cba,kba->bck', masked, harm_box, preferred_element_type=jnp.f...]
    mul x4 -> x0, other arithmetic: 12.3 us -> none  [body(): picked_block = ext_mult[:, :, index_block] * mask_block[None, None]]
    pallas_call x0 -> x1, Pallas kernels: none -> 11.9 us  [field(): pl.pallas_call(field_kernel, in_specs=[smem] * 3 + [vmem] * 6, out_specs=...]
    unnamed x32 -> x19, local copies, waits for them, and re-layouts: 1.75 us -> 11.6 us
    gather x8 -> x0, local copies, waits for them, and re-layouts: 9.16 us -> none  [the longest x7 5.65 us: body(): picked_block = ext_mult[:, :, index_block] * mask_block[None, None]]
    ppermute x2 -> x4, starting transfers between devices: 4.33 us -> 10.1 us  [the longest x1 4.5 us: body(): charge_low = lax.ppermute(flat_masked[:, atom_dev - ghost:], 'box', up)]
  transfers between devices with their start and end apart: 2 -> 4, of which waited for: 0 -> 0; matrix products, arithmetic and copies ran while one was open for 14% -> 10% of each run, Pallas kernels for 0% -> 0%
where the time goes in v2:
time: 138 us; the launch traced here: 137 us
  Pallas kernels  84.1 us (61%)
  blocking collectives  24.4 us (18%)
  local copies, waits for them, and re-layouts  14.6 us (11%)
  starting transfers between devices  10.1 us (7%)
  other arithmetic  2.52 us (2%)
  matrix products  1.49 us (1%)
    pallas_call x1, Pallas kernels, near_field(): pl.pallas_call(near_kernel, grid=(atoms // TILE,), in_specs=[pl.BlockSpec...  72.3 us
    all_gather x1, blocking collectives, body(): tops = lax.all_gather(top, 'box', axis=0, tiled=True)  24.4 us
    pallas_call x1, Pallas kernels, field(): pl.pallas_call(field_kernel, in_specs=[smem] * 3 + [vmem] * 6, out_specs=...  11.9 us
    unnamed x19, local copies, waits for them, and re-layouts  11.6 us
    ppermute x1, starting transfers between devices, body(): charge_low = lax.ppermute(flat_masked[:, atom_dev - ghost:], 'box', up)  4.5 us
    ppermute x1, starting transfers between devices, body(): rows_low = lax.ppermute(rows, 'box', up)  3.03 us
  transfers between devices with their start and end apart: 4, of which 0 were waited for; matrix products, arithmetic and copies ran while one was open for 10% of the time, Pallas kernels for 0%

profile of v2, /device:TPU:0, one launch (start us, length us, event | category | flops | bytes accessed | tf_op | source)
XLA Modules:
  0.0 137.5 jit_solution(1198955915146256272)
XLA Ops:
  0.0 0.8 iota_compare_fusion
  0.8 1.6 %copy.25 = bf16[16,8,8,512]{3,2,1,0:T(8,128)(2,1)S(1)} copy(bf16[16,8,8,512]{3,1,2,0:T(8,128)(2,1)} %bitcast.21) | data formatting | bytes 2097152
  2.4 0.1 slice.10
  2.5 1.3 convolution_convert_fusion
  3.8 1.3 collective-permute-start.1
  5.1 3.0 %collective-permute-start = (bf16[128,121]{1,0:T(8,128)(2,1)S(1)}, bf16[128,121]{1,0:T(8,128)(2,1)S(1)}, u32[]{:S(2)}, u32[]{:S(2)}) collective-permute-start(bf16[128,121]{1,0:T(8,128)(2,1)S(1)} %bitcast.24), channel_id=1, source_target_pairs={{0,1},{1,2},{2,3},{3,4},{4,5},{5,6},{6,7},{7,8},{8,9},{9,10},{10,1... | collective-permute-start | bytes 92936 | tf_op jit(solution)/shard_map/ppermute | solution.py:197
  8.2 0.7 lt.38
  8.9 0.9 broadcast_select_fusion
  9.9 4.5 %collective-permute-start.2 = (bf16[16,1024]{1,0:T(8,128)(2,1)S(1)}, bf16[16,1024]{1,0:T(8,128)(2,1)S(1)}, u32[]{:S(2)}, u32[]{:S(2)}) collective-permute-start(bf16[16,1024]{1,0:T(8,128)(2,1)S(1)} %get-tuple-element.5), channel_id=1, source_target_pairs={{0,1},{1,2},{2,3},{3,4},{4,5},{5,6},{6,7},{7,8},{8,9},{9,10},{10,1... | collective-permute-start | bytes 98312 | tf_op jit(solution)/shard_map/ppermute | solution.py:194
  14.4 1.3 collective-permute-start.3
  15.7 0.2 fusion
  15.9 1.3 dynamic-slice_bitcast_fusion
  17.2 0.1 copy.18
  17.3 0.7 reshape.39.source_ref
  18.0 0.8 copy.23.l2l_ref
  18.8 8.5 %copy.22.ops_ref = bf16[121,22869]{1,0:T(8,128)(2,1)} copy(bf16[121,22869]{0,1:T(8,128)(2,1)} %param.15) | data formatting | bytes 11068596 | tf_op args[3]
  27.3 24.4 %all_gather.3.tops_ref = bf16[256,121]{1,0:T(8,128)(2,1)} all-gather(bf16[16,121]{1,0:T(8,128)(2,1)S(1)} %fusion), channel_id=1, replica_groups=mesh['sys'=2,'box'=16] {'box'}, dimensions={0}, use_global_device_ids=true | all-gather | bytes 65824 | tf_op jit(solution)/shard_map/all_gather | solution.py:190
  51.7 0.0 collective-permute-done.1
  51.7 0.0 collective-permute-done
  51.7 0.8 maximum_maximum_fusion.table_ref
  52.5 0.1 reshape.43.table_ref
  52.6 72.3 %near_field.1.near_ref = f32[16,4096]{1,0:T(8,128)S(1)} custom-call(bf16[384,256]{1,0:T(8,128)(2,1)S(1)} %reshape.43.table_ref, s32[32,4096]{1,0:T(8,128)S(1)} %copy-done.2, bf16[32,4096]{1,0:T(8,128)(2,1)S(1)} %copy-done.3), custom_call_target="tpu_custom_call" | custom-call | flops 25769803776 | bytes 786432 | tf_op jit(solution)/shard_map/near_field/pallas_call | solution.py:41
  124.9 0.7 copy-done.1
  125.6 11.9 %field.1 = bf16[16,4096]{1,0:T(8,128)(2,1)} custom-call(s32[1512]{0:T(1024)} %reshape.39.source_ref, s32[32]{0:T(128)} %get-tuple-element.8.top_source_ref, s32[32]{0:T(128)} %get-tuple-element.7.top_vector_ref, bf16[400,121]{1,0:T(8,128)(2,1)} %maximum_maximum_fusion.table_ref, bf16[256,121]{1,0:T(8,128)(2,1)} %all_gather.3.tops_ref, ...), custom_call_target="tpu_custom_call" | custom-call | flops 796938880 | bytes 6525530 | tf_op jit(solution)/shard_map/field/pallas_call | solution.py:139
  (23 shorter events, 0.1 us)
Async XLA Ops:
  0.0 15.7 %copy-start = (bf16[8,121,121]{2,0,1:T(8,128)(2,1)S(1)}, bf16[8,121,121]{2,0,1:T(8,128)(2,1)}, u32[]{:S(2)}) copy-start(bf16[8,121,121]{2,0,1:T(8,128)(2,1)} %param.16) | copy-start | bytes 702772
  0.0 15.9 %copy-start.6 = (s32[189,8]{0,1:T(8,128)S(1)}, s32[189,8]{0,1:T(8,128)}, u32[]{:S(2)}) copy-start(s32[189,8]{0,1:T(8,128)} %param.19) | copy-start | bytes 18148
  0.0 15.9 %copy-start.5 = (s32[189,8]{0,1:T(8,128)S(1)}, s32[189,8]{0,1:T(8,128)}, u32[]{:S(2)}) copy-start(s32[189,8]{0,1:T(8,128)} %param.18) | copy-start | bytes 18148
  0.0 18.0 %copy-start.4 = (bf16[8,121,121]{2,0,1:T(8,128)(2,1)S(1)}, bf16[8,121,121]{2,0,1:T(8,128)(2,1)}, u32[]{:S(2)}) copy-start(bf16[8,121,121]{2,0,1:T(8,128)(2,1)} %param.17) | copy-start | bytes 702772
  3.8 47.9 %collective-permute-start.1 = (bf16[128,121]{1,0:T(8,128)(2,1)S(1)}, bf16[128,121]{1,0:T(8,128)(2,1)S(1)}, u32[]{:S(2)}, u32[]{:S(2)}) collective-permute-start(bf16[128,121]{1,0:T(8,128)(2,1)S(1)} %bitcast.23), channel_id=1, source_target_pairs={{1,0},{2,1},{3,2},{4,3},{5,4},{6,5},{7,6},{8,7},{9,8},{10,9},{11,1... | collective-permute-start | bytes 92936 | tf_op jit(solution)/shard_map/ppermute | solution.py:198
  5.1 46.6 %collective-permute-start = (bf16[128,121]{1,0:T(8,128)(2,1)S(1)}, bf16[128,121]{1,0:T(8,128)(2,1)S(1)}, u32[]{:S(2)}, u32[]{:S(2)}) collective-permute-start(bf16[128,121]{1,0:T(8,128)(2,1)S(1)} %bitcast.24), channel_id=1, source_target_pairs={{0,1},{1,2},{2,3},{3,4},{4,5},{5,6},{6,7},{7,8},{8,9},{9,10},{10,1... | collective-permute-start | bytes 92936 | tf_op jit(solution)/shard_map/ppermute | solution.py:197
  9.9 42.6 %collective-permute-start.2 = (bf16[16,1024]{1,0:T(8,128)(2,1)S(1)}, bf16[16,1024]{1,0:T(8,128)(2,1)S(1)}, u32[]{:S(2)}, u32[]{:S(2)}) collective-permute-start(bf16[16,1024]{1,0:T(8,128)(2,1)S(1)} %get-tuple-element.5), channel_id=1, source_target_pairs={{0,1},{1,2},{2,3},{3,4},{4,5},{5,6},{6,7},{7,8},{8,9},{9,10},{10,1... | collective-permute-start | bytes 98312 | tf_op jit(solution)/shard_map/ppermute | solution.py:194
  14.4 38.1 %collective-permute-start.3 = (bf16[16,1024]{1,0:T(8,128)(2,1)S(1)}, bf16[16,1024]{1,0:T(8,128)(2,1)S(1)}, u32[]{:S(2)}, u32[]{:S(2)}) collective-permute-start(bf16[16,1024]{1,0:T(8,128)(2,1)S(1)} %get-tuple-element.6), channel_id=1, source_target_pairs={{1,0},{2,1},{3,2},{4,3},{5,4},{6,5},{7,6},{8,7},{9,8},{10,9},{11,1... | collective-permute-start | bytes 98312 | tf_op jit(solution)/shard_map/ppermute | solution.py:195
  18.8 33.8 %copy-start.2 = (s32[32,4096]{1,0:T(8,128)S(1)}, s32[32,4096]{1,0:T(8,128)}, u32[]{:S(2)}) copy-start(s32[32,4096]{1,0:T(8,128)} %index_ref.1) | copy-start | bytes 1572868
  18.8 33.8 %copy-start.3 = (bf16[32,4096]{1,0:T(8,128)(2,1)S(1)}, bf16[32,4096]{1,0:T(8,128)(2,1)}, u32[]{:S(2)}) copy-start(bf16[32,4096]{1,0:T(8,128)(2,1)} %weight_ref.1) | copy-start | bytes 786436
  124.9 0.7 copy-start.1

commit v3 on v2

--- a/solution.py
+++ b/solution.py
@@ -57,6 +57,120 @@
     )(table, neighbours, edge_weights)
 
 
+def exchange_kernel(
+    top_ref,
+    rows_ref,
+    first_ref,
+    last_ref,
+    tops_ref,
+    rows_low_ref,
+    rows_high_ref,
+    charge_low_ref,
+    charge_high_ref,
+    top_send,
+    top_recv,
+    edge_send,
+    edge_recv,
+):
+    devices = lax.axis_size("box")
+    me = lax.axis_index("box")
+    part = lax.axis_index("sys")
+    chans = top_ref.shape[0]
+    mesh_ids = pl.DeviceIdType.MESH
+    barrier = pltpu.get_barrier_semaphore()
+
+    def greet(step, carry):
+        peer = lax.rem(me + step, devices)
+        pl.semaphore_signal(barrier, inc=1, device_id=(part, peer), device_id_type=mesh_ids)
+        return carry
+
+    lax.fori_loop(1, devices, greet, 0)
+    pl.semaphore_wait(barrier, devices - 1)
+
+    right = lax.rem(me + 1, devices)
+    left = lax.rem(me + devices - 1, devices)
+    edges = []
+    for spot, (source, target, peer) in enumerate(
+        (
+            (rows_ref, rows_low_ref, right),
+            (rows_ref, rows_high_ref, left),
+            (last_ref, charge_low_ref, right),
+            (first_ref, charge_high_ref, left),
+        )
+    ):
+        edges.append(
+            pltpu.make_async_remote_copy(
+                src_ref=source,
+                dst_ref=target,
+                send_sem=edge_send.at[spot],
+                recv_sem=edge_recv.at[spot],
+                device_id=(part, peer),
+                device_id_type=mesh_ids,
+            )
+        )
+
+    def top_copy(step):
+        peer = lax.rem(me + step, devices)
+        return pltpu.make_async_remote_copy(
+            src_ref=top_ref,
+            dst_ref=tops_ref.at[pl.ds(pl.multiple_of(me * chans, chans), chans)],
+            send_sem=top_send.at[step],
+            recv_sem=top_recv.at[step],
+            device_id=(part, peer),
+            device_id_type=mesh_ids,
+        )
+
+    def send(step, carry):
+        top_copy(step).start()
+        return carry
+
+    def receive(step, carry):
+        origin = lax.rem(me + devices - step, devices)
+        pltpu.make_async_remote_copy(
+            src_ref=top_ref,
+            dst_ref=tops_ref.at[pl.ds(pl.multiple_of(origin * chans, chans), chans)],
+            send_sem=top_send.at[step],
+            recv_sem=top_recv.at[step],
+            device_id=(part, lax.rem(me + step, devices)),
+            device_id_type=mesh_ids,
+        ).wait()
+        return carry
+
+    for copy in edges:
+        copy.start()
+    lax.fori_loop(1, devices, send, 0)
+    tops_ref[pl.ds(pl.multiple_of(me * chans, chans), chans), :] = top_ref[...]
+    for copy in edges:
+        copy.wait()
+    lax.fori_loop(1, devices, receive, 0)
+
+
+def exchange(top, rows, first, last):
+    devices = lax.axis_size("box")
+    chans, width = top.shape
+    vmem = pl.BlockSpec(memory_space=pltpu.VMEM)
+    return pl.pallas_call(
+        exchange_kernel,
+        in_specs=[vmem] * 4,
+        out_specs=[vmem] * 5,
+        out_shape=[
+            jax.ShapeDtypeStruct((devices * chans, width), jnp.bfloat16),
+            jax.ShapeDtypeStruct(rows.shape, jnp.bfloat16),
+            jax.ShapeDtypeStruct(rows.shape, jnp.bfloat16),
+            jax.ShapeDtypeStruct(last.shape, jnp.bfloat16),
+            jax.ShapeDtypeStruct(first.shape, jnp.bfloat16),
+        ],
+        scratch_shapes=[
+            pltpu.SemaphoreType.DMA((devices,)),
+            pltpu.SemaphoreType.DMA((devices,)),
+            pltpu.SemaphoreType.DMA((4,)),
+            pltpu.SemaphoreType.DMA((4,)),
+        ],
+        compiler_params=pltpu.CompilerParams(collective_id=0, has_side_effects=True),
+        name="exchange",
+    )(top, rows, first, last)
+
+
 CHUNK = 2048
 
 
@@ -75,15 +189,14 @@
     tops,
     stack,
 ):
-    ncoef, columns = ops_ref.shape
+    columns, ncoef = ops_ref.shape
     chans, atoms = out_ref.shape
     nvec = columns // ncoef
     boxes = source_ref.shape[0] // nvec
     leaf_rows = boxes * chans
     slots = atoms // boxes
-    table[:, :ncoef] = table_ref[...].astype(jnp.float32)
-    tops[...] = jnp.zeros_like(tops)
-    tops[:, :ncoef] = tops_ref[...].astype(jnp.float32)
+    table[...] = table_ref[...].astype(jnp.float32)
+    tops[...] = tops_ref[...].astype(jnp.float32)
     for vec in range(nvec):
         for box in range(boxes):
             row = pl.multiple_of(source_ref[vec * boxes + box] * chans, chans)
@@ -105,16 +218,18 @@
         return carry
 
     lax.fori_loop(0, top_source_ref.shape[0], add_entry, 0)
-    total = jnp.zeros((leaf_rows + chans, ncoef), jnp.float32)
+    total = jnp.zeros((leaf_rows + 2 * chans, ncoef), jnp.float32)
     for start in range(0, columns, CHUNK):
         stop = min(start + CHUNK, columns)
-        total = total + lax.dot_general(
-            stack[:, start:stop].astype(jnp.bfloat16),
-            ops_ref[:, start:stop],
-            (((1,), (1,)), ((), ())),
+        values = stack[:, start:stop]
+        high = values.astype(jnp.bfloat16)
+        rest = (values[leaf_rows:] - high[leaf_rows:].astype(jnp.float32)).astype(jnp.bfloat16)
+        total = total + jnp.dot(
+            jnp.concatenate([high, rest], axis=0),
+            ops_ref[start:stop, :],
             preferred_element_type=jnp.float32,
         )
-    parent = total[leaf_rows:].astype(jnp.bfloat16)
+    parent = (total[leaf_rows : leaf_rows + chans] + total[leaf_rows + chans :]).astype(jnp.bfloat16)
     for box in range(boxes):
         child = lax.dot_general(
             parent,
@@ -130,7 +245,7 @@
 
 def field(source, top_source, top_vector, table, tops, ops, l2l_ops, harmonics, near):
     chans, atoms = near.shape
-    ncoef, columns = ops.shape
+    columns, ncoef = ops.shape
     boxes = l2l_ops.shape[0]
     rows = (boxes + 1) * chans
     width = (columns // 128 + 2) * 128
@@ -187,26 +302,26 @@
     top = jnp.einsum("ocl,okl->ck", mult, m2m_ops, preferred_element_type=jnp.float32).astype(
         jnp.bfloat16
     )
-    tops = lax.all_gather(top, "box", axis=0, tiled=True)
-    devices = lax.axis_size("box")
-    up = [(i, (i + 1) % devices) for i in range(devices - 1)]
-    down = [(j, i) for i, j in up]
-    charge_low = lax.ppermute(flat_masked[:, atom_dev - ghost :], "box", up)
-    charge_high = lax.ppermute(flat_masked[:, :ghost], "box", down)
     rows = mult.reshape(box_dev * chans, ncoef)
-    rows_low = lax.ppermute(rows, "box", up)
-    rows_high = lax.ppermute(rows, "box", down)
+    rows = jnp.pad(rows, ((0, 0), (0, 128 - ncoef)))
+    top = jnp.pad(top, ((0, 0), (0, 128 - ncoef)))
+    tops, rows_low, rows_high, charge_low, charge_high = exchange(
+        top, rows, flat_masked[:, :ghost], flat_masked[:, atom_dev - ghost :]
+    )
+    last = lax.axis_size("box") - 1
+    charge_low = jnp.where(position == 0, jnp.zeros((), jnp.bfloat16), charge_low)
+    charge_high = jnp.where(position == last, jnp.zeros((), jnp.bfloat16), charge_high)
     ext_charges = jnp.concatenate([charge_low, flat_masked, charge_high], axis=1)
     near = near_field(ext_charges, neighbours, edge_weights)
     table = jnp.concatenate(
-        [rows_low, rows, rows_high, jnp.zeros((chans, ncoef), jnp.bfloat16)], axis=0
+        [rows_low, rows, rows_high, jnp.zeros((chans, 128), jnp.bfloat16)], axis=0
     )
     local_index = sources - (position - 1) * box_dev
     local_index = jnp.where(list_mask != 0, local_index, 3 * box_dev).reshape(-1)
     row_sources = lax.dynamic_slice_in_dim(top_sources, position, 1, 0)[0]
     row_vectors = lax.dynamic_slice_in_dim(top_vectors, position, 1, 0)[0]
     return field(
-        local_index, row_sources, row_vectors, table, tops, m2l_ops, l2l_ops, harmonics, near
+        local_index, row_sources, row_vectors, table, tops, m2l_ops.T, l2l_ops, harmonics, near
     )
 
 

time: 138 us -> 109 us (0.79)
  blocking collectives: 24.4 us -> 0 us
  Pallas kernels: 84.1 us -> 95.8 us
  starting transfers between devices: 10.1 us -> 0 us
  local copies, waits for them, and re-layouts: 14.6 us -> 8.06 us
    all_gather x1 -> x0, blocking collectives: 24.4 us -> none  [body(): tops = lax.all_gather(top, 'box', axis=0, tiled=True)]
    pallas_call x0 -> x1, Pallas kernels: none -> 11.4 us  [exchange(): pl.pallas_call(exchange_kernel, in_specs=[vmem] * 4, out_specs=[vmem] * 5...]
    ppermute x4 -> x0, starting transfers between devices: 10.1 us -> none  [the longest x1 4.5 us: body(): charge_low = lax.ppermute(flat_masked[:, atom_dev - ghost:], 'box', up)]
    unnamed x19 -> x24, local copies, waits for them, and re-layouts: 11.6 us -> 3.2 us
  transfers between devices with their start and end apart: 4 -> 0, of which waited for: 0 -> 0; matrix products, arithmetic and copies ran while one was open for 10% -> 0% of each run, Pallas kernels for 0% -> 0%
where the time goes in v3:
time: 109 us
  Pallas kernels  95.8 us (88%)
  local copies, waits for them, and re-layouts  8.06 us (7%)
  other arithmetic  3.22 us (3%)
  matrix products  1.48 us (1%)
    pallas_call x1, Pallas kernels, near_field(): pl.pallas_call(near_kernel, grid=(atoms // TILE,), in_specs=[pl.BlockSpec...  72.3 us
    pallas_call x1, Pallas kernels, field(): pl.pallas_call(field_kernel, in_specs=[smem] * 3 + [vmem] * 6, out_specs=...  12.2 us
    pallas_call x1, Pallas kernels, exchange(): pl.pallas_call(exchange_kernel, in_specs=[vmem] * 4, out_specs=[vmem] * 5...  11.4 us
    unnamed x24, local copies, waits for them, and re-layouts  3.2 us

profile of v3, /device:TPU:0, one launch (start us, length us, event | category | flops | bytes accessed | tf_op | source)
XLA Modules:
  0.0 108.8 jit_solution(14734633030511545825)
XLA Ops:
  0.0 1.7 %copy.23 = bf16[16,8,8,512]{3,2,1,0:T(8,128)(2,1)S(1)} copy(bf16[16,8,8,512]{3,1,2,0:T(8,128)(2,1)} %bitcast.23) | data formatting | bytes 2097152
  1.7 0.1 slice.10
  1.8 0.7 iota_compare_fusion
  2.5 1.3 %convolution_convert_fusion = bf16[8,16,121]{2,1,0:T(8,128)(2,1)S(1)} fusion(bf16[121,8,512]{2,1,0:T(8,128)(2,1)S(1)} %slice.10, bf16[2,8,8,512]{3,2,1,0:T(8,128)(2,1)} %bitcast.26, pred[8,512]{1,0:T(8,128)(4,1)S(1)} %iota_compare_fusion), kind=kOutput, calls=%fused_computation | convolution fusion | flops 15940736 | bytes 1157376 | tf_op jit(solution)/shard_map/cba,kba->bck/dot_general | solution.py:299
  3.8 0.6 pad.9.rows_ref
  4.5 0.7 lt.38
  5.2 0.9 broadcast_select_fusion
  6.1 0.6 fusion.7
  6.8 0.2 fusion
  6.9 0.6 pad.8.top_ref
  7.6 11.4 %exchange.1 = (bf16[256,128]{1,0:T(8,128)(2,1)}, bf16[128,128]{1,0:T(8,128)(2,1)}, bf16[128,128]{1,0:T(8,128)(2,1)}, bf16[16,1024]{1,0:T(8,128)(2,1)}, bf16[16,1024]{1,0:T(8,128)(2,1)}) custom-call(bf16[16,128]{1,0:T(8,128)(2,1)} %pad.8.top_ref, bf16[128,128]{1,0:T(8,128)(2,1)} %pad.9.rows_ref, bf16[16,1024]{1,0:T(8,128)(2,1)} %get-tuple-element.16.first_ref, ...), custom_call_target="tpu_custom_call" | custom-call | tf_op jit(solution)/shard_map/exchange/pallas_call | solution.py:152
  19.0 0.8 broadcast_select_fusion.1
  19.8 0.1 reshape.43.table_ref
  19.9 0.0 copy-start.4
  19.9 0.0 copy-start.8
  20.0 0.0 copy-start.9
  20.0 72.3 %near_field.1.near_ref = f32[16,4096]{1,0:T(8,128)S(1)} custom-call(bf16[384,256]{1,0:T(8,128)(2,1)S(1)} %reshape.43.table_ref, s32[32,4096]{1,0:T(8,128)S(1)} %copy-done.2, bf16[32,4096]{1,0:T(8,128)(2,1)S(1)} %copy-done.3), custom_call_target="tpu_custom_call" | custom-call | flops 25769803776 | bytes 786432 | tf_op jit(solution)/shard_map/near_field/pallas_call | solution.py:41
  92.3 0.7 copy-done.1
  93.0 0.8 maximum_maximum_fusion.table_ref
  93.8 1.3 %dynamic-slice_bitcast_fusion = (s32[32]{0:T(128)}, s32[32]{0:T(128)}) fusion(s32[16,32]{1,0:T(8,128)} %param.21, s32[]{:T(128)S(6)} %select_n.30, s32[16,32]{1,0:T(8,128)} %param.20), kind=kLoop, calls=%fused_computation.17 | loop fusion | bytes 516 | tf_op jit(solution)/shard_map/squeeze | solution.py:322
  95.0 0.1 copy.17
  95.2 0.7 reshape.39.source_ref
  95.9 0.7 copy.21.l2l_ref
  96.6 12.2 %field.1 = bf16[16,4096]{1,0:T(8,128)(2,1)} custom-call(s32[1512]{0:T(1024)} %reshape.39.source_ref, s32[32]{0:T(128)} %get-tuple-element.18.top_source_ref, s32[32]{0:T(128)} %get-tuple-element.17.top_vector_ref, bf16[400,128]{1,0:T(8,128)(2,1)} %maximum_maximum_fusion.table_ref, bf16[256,128]{1,0:T(8,128)(2,1)} %get-tuple-element.12.tops_ref, ...), custom_call_target="tpu_custom_call" | custom-call | flops 796938880 | bytes 6525530 | tf_op jit(solution)/shard_map/field/pallas_call | solution.py:254
  (23 shorter events, 0.1 us)
Async XLA Ops:
  0.0 6.8 %copy-start = (bf16[8,121,121]{2,0,1:T(8,128)(2,1)S(1)}, bf16[8,121,121]{2,0,1:T(8,128)(2,1)}, u32[]{:S(2)}) copy-start(bf16[8,121,121]{2,0,1:T(8,128)(2,1)} %param.16) | copy-start | bytes 702772
  0.0 19.9 %copy-start.2 = (s32[32,4096]{1,0:T(8,128)S(1)}, s32[32,4096]{1,0:T(8,128)}, u32[]{:S(2)}) copy-start(s32[32,4096]{1,0:T(8,128)} %index_ref.1) | copy-start | bytes 1572868
  0.0 19.9 %copy-start.3 = (bf16[32,4096]{1,0:T(8,128)(2,1)S(1)}, bf16[32,4096]{1,0:T(8,128)(2,1)}, u32[]{:S(2)}) copy-start(bf16[32,4096]{1,0:T(8,128)(2,1)} %weight_ref.1) | copy-start | bytes 786436
  19.9 73.1 %copy-start.4 = (bf16[128,128]{1,0:T(8,128)(2,1)S(1)}, bf16[128,128]{1,0:T(8,128)(2,1)}, u32[]{:S(2)}) copy-start(bf16[128,128]{1,0:T(8,128)(2,1)} %pad.9.rows_ref) | copy-start | bytes 98308
  19.9 73.1 %copy-start.6 = (bf16[128,128]{1,0:T(8,128)(2,1)S(1)}, bf16[128,128]{1,0:T(8,128)(2,1)}, u32[]{:S(2)}) copy-start(bf16[128,128]{1,0:T(8,128)(2,1)} %get-tuple-element.10) | copy-start | bytes 98308
  19.9 73.1 %copy-start.7 = (bf16[128,128]{1,0:T(8,128)(2,1)S(1)}, bf16[128,128]{1,0:T(8,128)(2,1)}, u32[]{:S(2)}) copy-start(bf16[128,128]{1,0:T(8,128)(2,1)} %get-tuple-element.11) | copy-start | bytes 98308
  19.9 75.1 %copy-start.8 = (s32[189,8]{0,1:T(8,128)S(1)}, s32[189,8]{0,1:T(8,128)}, u32[]{:S(2)}) copy-start(s32[189,8]{0,1:T(8,128)} %param.18) | copy-start | bytes 18148
  20.0 75.1 %copy-start.9 = (s32[189,8]{0,1:T(8,128)S(1)}, s32[189,8]{0,1:T(8,128)}, u32[]{:S(2)}) copy-start(s32[189,8]{0,1:T(8,128)} %param.19) | copy-start | bytes 18148
  20.0 75.9 %copy-start.5 = (bf16[8,121,121]{2,0,1:T(8,128)(2,1)S(1)}, bf16[8,121,121]{2,0,1:T(8,128)(2,1)}, u32[]{:S(2)}) copy-start(bf16[8,121,121]{2,0,1:T(8,128)(2,1)} %param.17) | copy-start | bytes 702772
  92.3 0.7 copy-start.1

commit v4 on v3

--- a/solution.py
+++ b/solution.py
@@ -7,7 +7,7 @@
 
 
 HI = 256
-TILE = 256
+TILE = 512
 
 
 def near_kernel(table_ref, index_ref, weight_ref, out_ref, weight_f32):
@@ -30,7 +30,7 @@
         terms = got.reshape(chans, groups // 8, 8, tile) * scale.reshape(1, groups // 8, 8, tile)
         return total + jnp.sum(terms, axis=1)
 
-    total = lax.fori_loop(0, slots, step, jnp.zeros((chans, 8, tile), jnp.float32), unroll=2)
+    total = lax.fori_loop(0, slots, step, jnp.zeros((chans, 8, tile), jnp.float32), unroll=True)
     out_ref[...] = jnp.sum(total, axis=1)
 
 

time: 109 us -> 65.5 us (0.60)
  Pallas kernels: 95.8 us -> 52.2 us
    pallas_call x1, Pallas kernels: 72.3 us -> 28.6 us  [near_field(): pl.pallas_call(near_kernel, grid=(atoms // TILE,), in_specs=[pl.BlockSpec...]
where the time goes in v4:
time: 65.5 us; the launch traced here: 65.1 us
  Pallas kernels  52.2 us (80%)
  local copies, waits for them, and re-layouts  8.06 us (12%)
  other arithmetic  3.22 us (5%)
  matrix products  1.48 us (2%)
    pallas_call x1, Pallas kernels, near_field(): pl.pallas_call(near_kernel, grid=(atoms // TILE,), in_specs=[pl.BlockSpec...  28.6 us
    pallas_call x1, Pallas kernels, field(): pl.pallas_call(field_kernel, in_specs=[smem] * 3 + [vmem] * 6, out_specs=...  12.1 us
    pallas_call x1, Pallas kernels, exchange(): pl.pallas_call(exchange_kernel, in_specs=[vmem] * 4, out_specs=[vmem] * 5...  11.4 us
    unnamed x24, local copies, waits for them, and re-layouts  3.2 us

profile of v4, /device:TPU:0, one launch (start us, length us, event | category | flops | bytes accessed | tf_op | source)
XLA Modules:
  0.0 65.1 jit_solution(15682496166794788035)
XLA Ops:
  0.0 1.7 %copy.23 = bf16[16,8,8,512]{3,2,1,0:T(8,128)(2,1)S(1)} copy(bf16[16,8,8,512]{3,1,2,0:T(8,128)(2,1)} %bitcast.23) | data formatting | bytes 2097152
  1.7 0.1 slice.10
  1.8 0.7 %iota_compare_fusion = pred[8,512]{1,0:T(8,128)(4,1)S(1)} fusion(s32[8]{0:T(128)} %param.14), kind=kLoop, calls=%fused_computation.15 | loop fusion | flops 4096 | bytes 4128 | tf_op jit(solution)/shard_map/lt | solution.py:293
  2.5 1.3 %convolution_convert_fusion = bf16[8,16,121]{2,1,0:T(8,128)(2,1)S(1)} fusion(bf16[121,8,512]{2,1,0:T(8,128)(2,1)S(1)} %slice.10, bf16[2,8,8,512]{3,2,1,0:T(8,128)(2,1)} %bitcast.26, pred[8,512]{1,0:T(8,128)(4,1)S(1)} %iota_compare_fusion), kind=kOutput, calls=%fused_computation | convolution fusion | flops 15940736 | bytes 1157376 | tf_op jit(solution)/shard_map/cba,kba->bck/dot_general | solution.py:299
  3.8 0.6 pad.9.rows_ref
  4.5 0.7 %lt.38 = s32[8,1,512]{2,1,0:T(1,128)S(1)} broadcast(s32[8]{0:T(128)} %param.14), dimensions={0} | broadcast | bytes 16416 | tf_op jit(solution)/shard_map/lt | solution.py:293
  5.2 0.9 %broadcast_select_fusion = bf16[16,4096]{1,0:T(8,128)(2,1)S(1)} fusion(bf16[16,4096]{1,0:T(8,128)(2,1)} %param.12, pred[4096]{0:T(1024)(128)(4,1)S(1)} %lt.40), kind=kLoop, calls=%fused_computation.8 | loop fusion | flops 65536 | bytes 266240 | tf_op jit(solution)/shard_map/jit(_where)/select_n | solution.py:294
  6.1 0.6 fusion.7
  6.8 0.2 fusion
  6.9 0.6 pad.8.top_ref
  7.6 11.4 %exchange.1 = (bf16[256,128]{1,0:T(8,128)(2,1)}, bf16[128,128]{1,0:T(8,128)(2,1)}, bf16[128,128]{1,0:T(8,128)(2,1)}, bf16[16,1024]{1,0:T(8,128)(2,1)}, bf16[16,1024]{1,0:T(8,128)(2,1)}) custom-call(bf16[16,128]{1,0:T(8,128)(2,1)} %pad.8.top_ref, bf16[128,128]{1,0:T(8,128)(2,1)} %pad.9.rows_ref, bf16[16,1024]{1,0:T(8,128)(2,1)} %get-tuple-element.16.first_ref, ...), custom_call_target="tpu_custom_call" | custom-call | tf_op jit(solution)/shard_map/exchange/pallas_call | solution.py:152
  19.0 0.8 %broadcast_select_fusion.1 = (bf16[16,1024]{1,0:T(8,128)(2,1)S(1)}, bf16[16,1024]{1,0:T(8,128)(2,1)S(1)}) fusion(bf16[16,1024]{1,0:T(8,128)(2,1)} %get-tuple-element.14, pred[]{:T(512)S(6)} %eq.7, bf16[16,1024]{1,0:T(8,128)(2,1)} %get-tuple-element.13, pred[]{:T(512)S(6)} %eq.6), kind=kLoop, calls=%fused_computation.12 | loop fusion | flops 32768 | bytes 131074 | tf_op jit(solution)/shard_map/jit(_where)/select_n | solution.py:313
  19.8 0.1 reshape.43.table_ref
  19.9 0.0 copy-start.4
  19.9 0.0 copy-start.8
  20.0 0.0 copy-start.9
  20.0 28.6 %near_field.1.near_ref = f32[16,4096]{1,0:T(8,128)S(1)} custom-call(bf16[384,256]{1,0:T(8,128)(2,1)S(1)} %reshape.43.table_ref, s32[32,4096]{1,0:T(8,128)S(1)} %copy-done.2, bf16[32,4096]{1,0:T(8,128)(2,1)S(1)} %copy-done.3), custom_call_target="tpu_custom_call" | custom-call | flops 25769803776 | bytes 786432 | tf_op jit(solution)/shard_map/near_field/pallas_call | solution.py:41
  48.6 0.7 %copy-done.1 = f32[16,4096]{1,0:T(8,128)} copy-done((f32[16,4096]{1,0:T(8,128)}, f32[16,4096]{1,0:T(8,128)S(1)}, u32[]{:S(2)}) %copy-start.1) | copy-done | bytes 262168
  49.3 0.8 %maximum_maximum_fusion.table_ref = bf16[400,128]{1,0:T(8,128)(2,1)} fusion(bf16[128,128]{1,0:T(8,128)(2,1)S(1)} %copy-done.7, bf16[128,128]{1,0:T(8,128)(2,1)S(1)} %copy-done.4, bf16[128,128]{1,0:T(8,128)(2,1)S(1)} %copy-done.6, bf16[400]{0:T(512)(128)(2,1)S(1)} %pad.16.clone), kind=kLoop, calls=%fused_computation.10 | loop fusion | flops 409600 | bytes 201504 | tf_op jit(solution)/shard_map/concatenate | solution.py:316
  50.1 1.3 %dynamic-slice_bitcast_fusion = (s32[32]{0:T(128)}, s32[32]{0:T(128)}) fusion(s32[16,32]{1,0:T(8,128)} %param.21, s32[]{:T(128)S(6)} %select_n.30, s32[16,32]{1,0:T(8,128)} %param.20), kind=kLoop, calls=%fused_computation.17 | loop fusion | bytes 516 | tf_op jit(solution)/shard_map/squeeze | solution.py:322
  51.4 0.1 copy.17
  51.5 0.7 %reshape.39.source_ref = s32[1512]{0:T(1024)} reshape(s32[189,8]{1,0:T(8,128)S(1)} %copy.17) | data formatting | bytes 12096 | tf_op jit(solution)/shard_map/reshape | solution.py:320
  52.2 0.7 %copy.21.l2l_ref = bf16[8,121,121]{2,1,0:T(8,128)(2,1)} copy(bf16[8,121,121]{2,0,1:T(8,128)(2,1)S(1)} %copy-done.5) | data formatting | bytes 468512 | tf_op args[5]
  52.9 12.1 %field.1 = bf16[16,4096]{1,0:T(8,128)(2,1)} custom-call(s32[1512]{0:T(1024)} %reshape.39.source_ref, s32[32]{0:T(128)} %get-tuple-element.18.top_source_ref, s32[32]{0:T(128)} %get-tuple-element.17.top_vector_ref, bf16[400,128]{1,0:T(8,128)(2,1)} %maximum_maximum_fusion.table_ref, bf16[256,128]{1,0:T(8,128)(2,1)} %get-tuple-element.12.tops_ref, ...), custom_call_target="tpu_custom_call" | custom-call | flops 796938880 | bytes 6525530 | tf_op jit(solution)/shard_map/field/pallas_call | solution.py:254
  (23 shorter events, 0.1 us)
Async XLA Ops:
  0.0 6.8 %copy-start = (bf16[8,121,121]{2,0,1:T(8,128)(2,1)S(1)}, bf16[8,121,121]{2,0,1:T(8,128)(2,1)}, u32[]{:S(2)}) copy-start(bf16[8,121,121]{2,0,1:T(8,128)(2,1)} %param.16) | copy-start | bytes 702772
  0.0 19.9 %copy-start.2 = (s32[32,4096]{1,0:T(8,128)S(1)}, s32[32,4096]{1,0:T(8,128)}, u32[]{:S(2)}) copy-start(s32[32,4096]{1,0:T(8,128)} %index_ref.1) | copy-start | bytes 1572868
  0.0 19.9 %copy-start.3 = (bf16[32,4096]{1,0:T(8,128)(2,1)S(1)}, bf16[32,4096]{1,0:T(8,128)(2,1)}, u32[]{:S(2)}) copy-start(bf16[32,4096]{1,0:T(8,128)(2,1)} %weight_ref.1) | copy-start | bytes 786436
  19.9 29.4 %copy-start.4 = (bf16[128,128]{1,0:T(8,128)(2,1)S(1)}, bf16[128,128]{1,0:T(8,128)(2,1)}, u32[]{:S(2)}) copy-start(bf16[128,128]{1,0:T(8,128)(2,1)} %pad.9.rows_ref) | copy-start | bytes 98308
  19.9 29.4 %copy-start.6 = (bf16[128,128]{1,0:T(8,128)(2,1)S(1)}, bf16[128,128]{1,0:T(8,128)(2,1)}, u32[]{:S(2)}) copy-start(bf16[128,128]{1,0:T(8,128)(2,1)} %get-tuple-element.10) | copy-start | bytes 98308
  19.9 29.4 %copy-start.7 = (bf16[128,128]{1,0:T(8,128)(2,1)S(1)}, bf16[128,128]{1,0:T(8,128)(2,1)}, u32[]{:S(2)}) copy-start(bf16[128,128]{1,0:T(8,128)(2,1)} %get-tuple-element.11) | copy-start | bytes 98308
  19.9 31.4 %copy-start.8 = (s32[189,8]{0,1:T(8,128)S(1)}, s32[189,8]{0,1:T(8,128)}, u32[]{:S(2)}) copy-start(s32[189,8]{0,1:T(8,128)} %param.18) | copy-start | bytes 18148
  20.0 31.4 %copy-start.9 = (s32[189,8]{0,1:T(8,128)S(1)}, s32[189,8]{0,1:T(8,128)}, u32[]{:S(2)}) copy-start(s32[189,8]{0,1:T(8,128)} %param.19) | copy-start | bytes 18148
  20.0 32.2 %copy-start.5 = (bf16[8,121,121]{2,0,1:T(8,128)(2,1)S(1)}, bf16[8,121,121]{2,0,1:T(8,128)(2,1)}, u32[]{:S(2)}) copy-start(bf16[8,121,121]{2,0,1:T(8,128)(2,1)} %param.17) | copy-start | bytes 702772
  48.6 0.7 %copy-start.1 = (f32[16,4096]{1,0:T(8,128)}, f32[16,4096]{1,0:T(8,128)S(1)}, u32[]{:S(2)}) copy-start(f32[16,4096]{1,0:T(8,128)S(1)} %near_field.1.near_ref) | copy-start | bytes 786436
